TPU v7x, 32 devices: a whole 2x2x4 slice. The times are simulated.
32 devices in a mesh: section: 2 (over y), shard: 16 (over z, x, core).
Axes of the slice: x: 2, y: 2, z: 4, core: 2. Of those that a mesh axis runs over, the one named last changes fastest.
Arguments:
- features: bfloat16 [2, 4096, 512], P(None, 'shard'), may hold values from -0.029907227 to 0.029907227
- labels: int32 [2, 4096], P(None, 'shard'), may hold values from 0 to 3
- label_table: float32 [4, 512], replicated, may hold values from -0.01 to 0.01
- tiles: bfloat16 [2, 96, 128, 128], P(None, 'shard'), may hold values from -1 to 1
- tile_rows: int32 [2, 96], P(None, 'shard'), may hold values from 0 to 31, as said below
- tile_cols: int32 [2, 96], P(None, 'shard'), may hold values from 0 to 31, as said below
- tile_live: int32 [2, 16], P(None, 'shard'), may hold values from 2 to 6, as said below
- weights: bfloat16 [2, 512, 512], P('section'), may hold values from -0.25 to 0.25
- gains: bfloat16 [2, 512], P('section'), may hold values from 0 to 1
- head_weight: float32 [512], replicated, may hold values from -0.75 to 0.75
Outputs:
- outcome: float32 [2, 4096], P('section', 'shard')
Inputs may be any that keep to these rules, and one draw needn't show every extreme that they name: `tile_rows`: slot k of shard j has a row block from j * 2 - 1 to (j + 1) * 2. `tile_cols`: slot k of shard j has a column block of that shard's own nodes, j * 2 to (j + 1) * 2 - 1; where its row block is j * 2 - 1 the column block is j * 2, and where its row block is (j + 1) * 2 the column block is (j + 1) * 2 - 1. `tile_live`: in every graph group some shard has all 6 slots live.
All inputs are finite; a program needn't handle non-finite values.
Results may differ from a plain program's by a relative error of at most 0.02.
Values may be sent and summed in bfloat16 or wider, within the bound.
No kernel may reach another device: no remote copies, remote signals or barrier semaphores. Data moves between devices by JAX's collectives and lax.ppermute only.
A program may use at most 64 MiB of HBM per device.

v0:
```python
import jax
import jax.numpy as jnp
from jax import lax
from jax.experimental import pallas as pl
from jax.experimental.pallas import tpu as pltpu
from jax.sharding import PartitionSpec as P

BF16 = jnp.bfloat16
F32 = jnp.float32
PAD = 16
EXTRA = 8
GELU_LINEAR = 2.0 * (2.0 / 3.141592653589793) ** 0.5
GELU_CUBIC = 4.0 * GELU_LINEAR * 0.044715


def split3(value):
    high = value.astype(BF16).astype(F32)
    rest = value - high
    mid = rest.astype(BF16).astype(F32)
    return high, mid, rest - mid


def dot(a, b, dims=((1,), (0,))):
    return lax.dot_general(a, b, (dims, ((), ())), preferred_element_type=F32)


def in_hbm(*arrays):
    return [pltpu.with_memory_space_constraint(array, pltpu.HBM) for array in arrays]


def layer(aggregate, weight, half_gain, state):
    projected = dot(aggregate, weight)
    scale = lax.rsqrt(jnp.mean(projected * projected, axis=-1, keepdims=True) + 1e-06)
    half = (projected * scale * half_gain).astype(BF16)
    inner = half * (BF16(GELU_LINEAR) + BF16(GELU_CUBIC) * (half * half))
    return state + (half + half * jnp.tanh(inner))


def placed(block, blocks, shard, size):
    mirrored = 1 - lax.rem(shard, 2)
    return pl.ds(pl.multiple_of((block + mirrored * (blocks - 1 - 2 * block)) * size, size), size)


def first_kernel(
    tile_rows, tile_cols, tile_live, labels, label_table, tiles, features, gains, weights,
    far, far_sum, near, crossing, state_out, adjacency_out,
    rows_buf, cols_buf, live_buf, labels_buf, classes_buf, tiles_buf, features_buf, gains_buf, table_buf, sums, sems,
):
    section = lax.axis_index("section")
    shard = lax.axis_index("shard")
    rows, width = features_buf.shape
    slots, size, _ = tiles_buf.shape
    blocks = rows // size
    kept = crossing.shape[0] - EXTRA
    group = section

    small = [(tile_rows, rows_buf), (tile_cols, cols_buf), (tile_live, live_buf)]
    named = [(label_table, classes_buf)]
    spread = []
    for block in range(blocks):
        span, place = pl.ds(block * size, size), placed(block, blocks, shard, size)
        named.append((labels.at[:, span], labels_buf.at[:, place]))
        spread.append((features.at[group, span], features_buf.at[place]))
    half = pl.ds(pl.multiple_of(lax.rem(shard, 2) * kept, kept), kept)
    sent = [(gains, gains_buf), (weights.at[0, half], crossing.at[pl.ds(0, kept)])]
    batches, count = [], 0
    for batch in (small, named, [(tiles.at[group], tiles_buf)], spread, sent):
        batches.append([
            pltpu.make_async_copy(source, target, sems.at[count + index])
            for index, (source, target) in enumerate(batch)
        ])
        count += len(batch)
    for batch in batches:
        for copy in batch:
            copy.start()
    sums[...] = jnp.zeros_like(sums)
    table_buf[...] = jnp.zeros_like(table_buf)

    for copy in batches[1]:
        copy.wait()
    classes = classes_buf.shape[0]
    for part, value in enumerate(split3(classes_buf[...])):
        table_buf[pl.ds(part * classes, classes), :] = value
    depth = table_buf.shape[0]
    index = lax.broadcasted_iota(jnp.int32, (depth, rows), 0)
    wanted = jnp.where(
        index < classes, index,
        jnp.where(index < 2 * classes, index - classes, jnp.where(index < 3 * classes, index - 2 * classes, -1)),
    )
    hot = (wanted == labels_buf[pl.ds(group, 1), :]).astype(F32).astype(BF16)
    embedded = dot(hot, table_buf[...].astype(BF16), ((0,), (0,)))

    for copy in batches[0] + batches[2]:
        copy.wait()
    for slot in range(slots):
        @pl.when(slot < live_buf[0, group])
        def _():
            row = rows_buf[group, slot] - (shard * blocks - 1)
            col = cols_buf[group, slot] - shard * blocks
            sums[placed(row, blocks + 2, shard, size), placed(col, blocks, shard, size)] += tiles_buf[slot].astype(F32)
    adjacency = sums[...].astype(BF16)
    adjacency_out[...] = adjacency

    for copy in batches[3]:
        copy.wait()
    state = (features_buf[...].astype(F32) + embedded).astype(BF16)
    state_out[...] = state
    partial = dot(adjacency[size : size + rows], state).astype(BF16)
    near[:, pl.ds(0, width)] = partial[:size]
    near[:, pl.ds(width, width)] = state[:size]
    near[:, pl.ds(2 * width, size)] = adjacency[:size, :size]
    far_sum[...] = partial[rows - size :]
    far[:, pl.ds(0, width)] = state[rows - size :]
    far[:, pl.ds(width, size)] = adjacency[rows + size :, rows - size :]
    batches[4][0].wait()
    crossing[pl.ds(kept, EXTRA), :] = jnp.broadcast_to(gains_buf[...].astype(F32), (EXTRA, width)).astype(BF16)
    batches[4][1].wait()


def waiting_kernel(
    adjacency, state, head, gains, weights,
    aggregate, weight, half_gain, head_row,
    gains_buf, sems,
):
    copies = [
        pltpu.make_async_copy(source, target, sems.at[index])
        for index, (source, target) in enumerate(((weights.at[0], weight), (head, head_row), (gains, gains_buf)))
    ]
    for copy in copies:
        copy.start()
    aggregate[...] = dot(adjacency[...], state[...])
    copies[2].wait()
    half_gain[...] = 0.5 * gains_buf[...].astype(F32)
    copies[0].wait()
    copies[1].wait()


def near_kernel(near, aggregate, state, weight, half_gain, near_blocks):
    size, width = near.shape[0], aggregate.shape[1]
    near_state = near[:, pl.ds(width, width)]
    first, second = pl.ds(0, size), pl.ds(size, size)
    near_blocks[first, :] = (aggregate[first, :] + near[:, pl.ds(0, width)].astype(F32)).astype(BF16)
    near_blocks[second, :] = (aggregate[second, :] + dot(near[:, pl.ds(2 * width, size)], near_state)).astype(BF16)

    @pl.when(lax.axis_index("section") == 0)
    def _():
        for span, before in ((first, near_state), (second, state[pl.ds(0, size), :])):
            near_blocks[span, :] = layer(near_blocks[span, :], weight[...], half_gain[...], before)


def far_kernel(far, near, near_blocks, aggregate, adjacency, state, weight, half_gain, far_blocks, inner, states):
    size = far.shape[0]
    rows, width = state.shape
    for start in range(0, rows - 2 * size, size):
        far_blocks[pl.ds(start, size), :] = aggregate[pl.ds(2 * size + start, size), :].astype(BF16)
    far_blocks[pl.ds(rows - 2 * size, size), :] = (
        aggregate[pl.ds(rows, size), :] + dot(far[:, pl.ds(width, size)], far[:, pl.ds(0, width)])
    ).astype(BF16)

    @pl.when(lax.axis_index("section") == 0)
    def _():
        for start in range(0, rows - size, size):
            span = pl.ds(start, size)
            far_blocks[span, :] = layer(
                far_blocks[span, :], weight[...], half_gain[...], state[pl.ds(size + start, size), :]
            )
        states[pl.ds(0, size), :] = near_blocks[pl.ds(size, size), :]
        states[pl.ds(size, rows - size), :] = far_blocks[...]
        inner[...] = dot(adjacency[pl.ds(size, rows), :], states[...])
        inner[pl.ds(0, size), :] += dot(near[:, pl.ds(2 * width, size)], near_blocks[pl.ds(0, size), :])


def second_kernel(*refs):
    first = lax.axis_index("section") == 0

    @pl.when(first)
    def _():
        both_layers(True, *refs)

    @pl.when(jnp.logical_not(first))
    def _():
        both_layers(False, *refs)


def both_layers(
    own_first,
    adjacency, state, far, far_sum, near, crossed, relayed, near_blocks, far_blocks, known_inner, aggregate,
    own_weight, half_gain, head_row,
    outcome,
    got_weight, next_states,
):
    shard = lax.axis_index("shard")
    even = lax.rem(shard, 2) == 0
    rows, width = state.shape
    size = near.shape[0]
    kept = crossed.shape[0] - EXTRA
    inside, last = pl.ds(size, rows), pl.ds(size + rows, size)

    for place, (one, two) in enumerate(((crossed, relayed), (relayed, crossed))):
        got_weight[pl.ds(place * kept, kept), :] = jnp.where(even, one[pl.ds(0, kept), :], two[pl.ds(0, kept), :])
    got_gain = 0.5 * crossed[pl.ds(kept, EXTRA), :].astype(F32)[0:1]
    used = ((own_weight, half_gain[...]), (got_weight, got_gain))
    (weight, gain), (last_weight, last_gain) = used if own_first else used[::-1]
    far_tile = far[:, pl.ds(width, size)]
    halo = (aggregate[last, :] + far_sum[...].astype(F32)).astype(BF16)

    if own_first:
        next_states[pl.ds(0, 2 * size), :] = near_blocks[...]
        next_states[pl.ds(2 * size, rows - size), :] = far_blocks[...]
    else:
        for start in range(0, rows, size):
            span = pl.ds(start, size)
            source = near_blocks[pl.ds(size, size), :] if start == 0 else far_blocks[pl.ds(start - size, size), :]
            next_states[pl.ds(size + start, size), :] = layer(source, weight[...], gain, state[span, :])
        next_states[pl.ds(0, size), :] = layer(
            near_blocks[pl.ds(0, size), :], weight[...], gain, near[:, pl.ds(width, width)]
        )
    next_states[last, :] = layer(halo, weight[...], gain, far[:, pl.ds(0, width)])

    if own_first:
        inner = known_inner[...]
    else:
        inner = dot(adjacency[inside, :], next_states[inside, :])
    for block in range(rows // size):
        start = block * size
        summed = inner[start : start + size]
        if block == 0 and not own_first:
            summed = summed + dot(near[:, pl.ds(2 * width, size)], next_states[pl.ds(0, size), :])
        if block == rows // size - 1:
            summed = summed + dot(far_tile, next_states[last, :])
        before = next_states[pl.ds(size + start, size), :]
        after = layer(summed.astype(BF16), last_weight[...], last_gain, before)
        weighted = after.astype(F32) * head_row[...]
        folded = weighted[:, :size]
        for at in range(size, width, size):
            folded = folded + weighted[:, at : at + size]
        outcome[:, placed(block, rows // size, shard, size)] = jnp.sum(folded.T, axis=0, keepdims=True)


def paired(features, labels, label_table, tiles, tile_rows, tile_cols, tile_live, weights, gains, head_weight):
    shard_count = lax.axis_size("shard")
    groups, rows, width = features.shape
    _, slots, size, _ = tiles.shape
    depth = weights.shape[1]
    kept = depth // 2
    classes = label_table.shape[0]
    message = jax.ShapeDtypeStruct((size, 2 * width + size), BF16)
    vmem = pl.BlockSpec(memory_space=pltpu.VMEM)
    hbm = pl.BlockSpec(memory_space=pltpu.HBM)
    table_rows = -(-3 * classes // PAD) * PAD

    far, far_sum, near, crossing, state, adjacency = pl.pallas_call(
        first_kernel,
        out_shape=(
            jax.ShapeDtypeStruct((size, width + size), BF16),
            jax.ShapeDtypeStruct((size, width), BF16),
            message,
            jax.ShapeDtypeStruct((kept + EXTRA, width), BF16),
            jax.ShapeDtypeStruct((rows, width), BF16),
            jax.ShapeDtypeStruct((rows + 2 * size, rows), BF16),
        ),
        in_specs=[hbm] * 9,
        out_specs=(vmem,) * 6,
        scratch_shapes=[
            pltpu.SMEM((groups, slots), jnp.int32),
            pltpu.SMEM((groups, slots), jnp.int32),
            pltpu.SMEM((1, groups), jnp.int32),
            pltpu.VMEM((groups, rows), jnp.int32),
            pltpu.VMEM((classes, width), F32),
            pltpu.VMEM((slots, size, size), BF16),
            pltpu.VMEM((rows, width), BF16),
            pltpu.VMEM((1, width), BF16),
            pltpu.VMEM((table_rows, width), F32),
            pltpu.VMEM((rows + 2 * size, rows), F32),
            pltpu.SemaphoreType.DMA((7 + 2 * (rows // size),)),
        ],
        compiler_params=pltpu.CompilerParams(vmem_limit_bytes=16 * 2**20),
        name="messages",
    )(*in_hbm(tile_rows, tile_cols, tile_live.T, labels, label_table, tiles, features, gains, weights))

    beside = [(i, i ^ 1) for i in range(shard_count)]
    apart = [(i, (i + 1) % shard_count) for i in range(1, shard_count, 2)]
    apart += [(b, a) for a, b in apart]
    across = [(0, 1), (1, 0)]
    crossed = lax.ppermute(crossing, "section", across)
    far = lax.ppermute(far, "shard", apart)
    far_sum = lax.ppermute(far_sum, "shard", [pair for pair in apart if abs(pair[0] - pair[1]) == 1])
    near = lax.ppermute(near, "shard", beside)

    aggregate, own_weight, half_gain, head_row = pl.pallas_call(
        waiting_kernel,
        out_shape=(
            jax.ShapeDtypeStruct((rows + 2 * size, width), F32),
            jax.ShapeDtypeStruct((depth, width), BF16),
            jax.ShapeDtypeStruct((1, width), F32),
            jax.ShapeDtypeStruct((1, width), F32),
        ),
        in_specs=[vmem] * 2 + [hbm] * 3,
        out_specs=(vmem,) * 4,
        scratch_shapes=[
            pltpu.VMEM((1, width), BF16),
            pltpu.SemaphoreType.DMA((3,)),
        ],
        compiler_params=pltpu.CompilerParams(vmem_limit_bytes=16 * 2**20),
        cost_estimate=pl.CostEstimate(flops=15 * 10**8, bytes_accessed=2**20, transcendentals=0),
        name="waiting",
    )(adjacency, state, *in_hbm(head_weight.reshape(1, width), gains, weights))

    near_blocks = pl.pallas_call(
        near_kernel,
        out_shape=jax.ShapeDtypeStruct((2 * size, width), BF16),
        in_specs=[vmem] * 5,
        out_specs=vmem,
        compiler_params=pltpu.CompilerParams(vmem_limit_bytes=16 * 2**20),
        name="beside",
    )(near, aggregate, state, own_weight, half_gain)

    crossed, near_blocks = lax.optimization_barrier((crossed, near_blocks))
    relayed = lax.ppermute(crossed, "shard", beside)

    far_blocks, inner = pl.pallas_call(
        far_kernel,
        out_shape=(
            jax.ShapeDtypeStruct((rows - size, width), BF16),
            jax.ShapeDtypeStruct((rows, width), F32),
        ),
        in_specs=[vmem] * 8,
        out_specs=(vmem,) * 2,
        scratch_shapes=[pltpu.VMEM((rows, width), BF16)],
        compiler_params=pltpu.CompilerParams(vmem_limit_bytes=16 * 2**20),
        cost_estimate=pl.CostEstimate(flops=4 * 10**9, bytes_accessed=2**20, transcendentals=0),
        name="apart",
    )(far, near, near_blocks, aggregate, adjacency, state, own_weight, half_gain)

    return pl.pallas_call(
        second_kernel,
        out_shape=jax.ShapeDtypeStruct((1, rows), F32),
        in_specs=[vmem] * 14,
        out_specs=vmem,
        scratch_shapes=[
            pltpu.VMEM((depth, width), BF16),
            pltpu.VMEM((rows + 2 * size, width), BF16),
        ],
        compiler_params=pltpu.CompilerParams(vmem_limit_bytes=32 * 2**20),
        name="layers",
    )(
        adjacency, state, far, far_sum, near, crossed, relayed, near_blocks, far_blocks, inner, aggregate,
        own_weight, half_gain, head_row,
    )


def extended_2(block, sides, width):
    for axis, dim in sides:
        count = lax.axis_size(axis)
        forward = [(i, i + 1) for i in range(count - 1)]
        backward = [(target, source) for source, target in forward]
        low = lax.ppermute(
            lax.slice_in_dim(block, block.shape[dim] - width, None, axis=dim), axis, forward
        )
        high = lax.ppermute(lax.slice_in_dim(block, 0, width, axis=dim), axis, backward)
        block = jnp.concatenate([low, block, high], axis=dim)
    return block


def body(
    features,
    labels,
    label_table,
    tiles,
    tile_rows,
    tile_cols,
    tile_live,
    weights,
    gains,
    head_weight,
):
    section_count = lax.axis_size("section")
    section_index = lax.axis_index("section")
    shard_index = lax.axis_index("shard")
    batch_count = features.shape[0]
    row_count = features.shape[1]
    feature_width = features.shape[2]
    tile_size = tiles.shape[2]
    slot_count = tiles.shape[1]
    label_count = label_table.shape[0]
    per_rows = row_count // tile_size
    per_section = batch_count // section_count
    slot_ids = jnp.arange(slot_count, dtype=jnp.int32)
    place_ids = jnp.arange(per_rows + 2, dtype=jnp.int32)

    def apply_layer(state, parts, layer_weight, layer_gain):
        group_tiles, col_local, placing, from_below, from_above = parts
        block_view = state.reshape(per_rows, tile_size, feature_width)
        chosen_blocks = jnp.take(block_view, col_local, axis=0)
        products = jnp.einsum(
            "kab,kbd->kad", group_tiles, chosen_blocks, preferred_element_type=jnp.float32
        )
        partial_value = jnp.einsum(
            "kp,kad->pad", placing, products, precision=lax.Precision.HIGHEST
        )
        edge_states = jnp.concatenate([state[:tile_size], state[row_count - tile_size :]], axis=0)
        extended = extended_2(edge_states, (("shard", 0),), tile_size)
        below_block = extended[:tile_size].astype(jnp.float32)
        above_block = extended[extended.shape[0] - tile_size :].astype(jnp.float32)
        own_rows = partial_value.reshape(row_count, feature_width)
        own_rows = own_rows.at[:tile_size].add(
            jnp.dot(from_below, below_block, precision=lax.Precision.HIGHEST)
        )
        own_rows = own_rows.at[row_count - tile_size :].add(
            jnp.dot(from_above, above_block, precision=lax.Precision.HIGHEST)
        )
        aggregate = own_rows.astype(jnp.bfloat16)
        projected = jnp.dot(aggregate, layer_weight, preferred_element_type=jnp.float32)
        scale = lax.rsqrt(jnp.mean(projected * projected, axis=-1, keepdims=True) + 1e-06)
        normed = projected * scale * layer_gain.astype(jnp.float32)
        return (state.astype(jnp.float32) + jax.nn.gelu(normed)).astype(jnp.bfloat16)

    layer_mats, layer_gains = (
        lax.all_gather(weights, "section", axis=0, tiled=True),
        lax.all_gather(gains, "section", axis=0, tiled=True),
    )
    batch_index = section_index * per_section + 0
    group_tiles = lax.dynamic_index_in_dim(tiles, batch_index, 0, keepdims=False)
    group_rows = lax.dynamic_index_in_dim(tile_rows, batch_index, 0, keepdims=False)
    group_cols = lax.dynamic_index_in_dim(tile_cols, batch_index, 0, keepdims=False)
    group_live = lax.dynamic_index_in_dim(tile_live, batch_index, 0, keepdims=False)
    col_local = group_cols - shard_index * per_rows
    slot_local = group_rows - (shard_index * per_rows - 1)
    live_mask = (slot_ids < group_live[0]).astype(jnp.float32)
    placing = (slot_local[:, None] == place_ids[None, :]).astype(jnp.float32) * live_mask[:, None]
    edge_pick = jnp.stack([placing[:, 0], placing[:, per_rows + 1]], axis=1)
    edge_tiles = jnp.einsum(
        "kp,kab->pab", edge_pick, group_tiles.astype(jnp.float32), precision=lax.Precision.HIGHEST
    )
    received = extended_2(edge_tiles, (("shard", 0),), 1)
    parts = (group_tiles, col_local, placing[:, 1 : per_rows + 1], received[0], received[3])

    def through(layer_index, state):
        return apply_layer(state, parts, layer_mats[layer_index], layer_gains[layer_index])

    group_labels = lax.dynamic_index_in_dim(labels, batch_index, 0, keepdims=False)
    group_features = lax.dynamic_index_in_dim(features, batch_index, 0, keepdims=False)
    labels_hot = (
        group_labels[:, None] == jnp.arange(label_count, dtype=jnp.int32)[None, :]
    ).astype(jnp.float32)
    embedded = jnp.dot(labels_hot, label_table, precision=lax.Precision.HIGHEST)
    state = lax.fori_loop(
        0,
        section_count,
        through,
        (group_features.astype(jnp.float32) + embedded).astype(jnp.bfloat16),
    )
    results = [jnp.dot(state.astype(jnp.float32), head_weight, precision=lax.Precision.HIGHEST)]
    return jnp.stack(results)


def solution(mesh):
    return jax.shard_map(
        paired if mesh.shape["section"] == 2 else body,
        mesh=mesh,
        in_specs=(
            P(None, "shard", None),
            P(None, "shard"),
            P(),
            P(None, "shard", None, None),
            P(None, "shard"),
            P(None, "shard"),
            P(None, "shard"),
            P("section", None, None),
            P("section", None),
            P(),
        ),
        out_specs=P("section", "shard"),
        check_vma=False,
    )
```

profile of v0, /device:TPU:0, one launch (start us, length us, event | category | flops | bytes accessed | tf_op | source)
XLA Modules:
  0.0 14.8 jit_solution(11314023304117134082)
XLA Ops:
  0.0 1.5 %messages.1 = (bf16[128,640]{1,0:T(8,128)(2,1)S(1)}, bf16[128,512]{1,0:T(8,128)(2,1)S(1)}, bf16[128,1152]{1,0:T(8,128)(2,1)S(1)}, bf16[264,512]{1,0:T(8,128)(2,1...) custom-call(s32[2,6]{1,0:T(2,128)} %tile_rows.1, s32[2,6]{1,0:T(2,128)} %tile_cols.1, s32[1,2]{1,0:T(1,128)} %bitcast.2, ...), custom_call_target="tpu_custom_call" | custom-call | tf_op jit(solution)/shard_map/messages/pallas_call | solution.py:252
  1.5 0.5 %collective-permute-start.2 = (bf16[128,1152]{1,0:T(8,128)(2,1)S(1)}, bf16[128,1152]{1,0:T(8,128)(2,1)S(1)}, u32[]{:S(2)}, u32[]{:S(2)}) collective-permute-start(bf16[128,1152]{1,0:T(8,128)(2,1)S(1)} %get-tuple-element.23), channel_id=1, source_target_pairs={{0,1},{1,0},{2,3},{3,2},{4,5},{5,4},{6,7},{7,6},{8,9},{9,8},{10,11... | collective-permute-start | bytes 884744 | tf_op jit(solution)/shard_map/ppermute | solution.py:288
  2.0 2.6 %collective-permute-start.3 = (bf16[264,512]{1,0:T(8,128)(2,1)S(1)}, bf16[264,512]{1,0:T(8,128)(2,1)S(1)}, u32[]{:S(2)}, u32[]{:S(2)}) collective-permute-start(bf16[264,512]{1,0:T(8,128)(2,1)S(1)} %get-tuple-element.24), channel_id=1, source_target_pairs={{0,16},{16,0},{1,17},{17,1},{2,18},{18,2},{3,19},{19,3},{4,20},{20... | collective-permute-start | bytes 811016 | tf_op jit(solution)/shard_map/ppermute | solution.py:285
  4.6 4.3 %collective-permute-start = (bf16[128,640]{1,0:T(8,128)(2,1)S(1)}, bf16[128,640]{1,0:T(8,128)(2,1)S(1)}, u32[]{:S(2)}, u32[]{:S(2)}) collective-permute-start(bf16[128,640]{1,0:T(8,128)(2,1)S(1)} %get-tuple-element.21), channel_id=1, source_target_pairs={{1,2},{3,4},{5,6},{7,8},{9,10},{11,12},{13,14},{15,0},{2,1},{4,3},... | collective-permute-start | bytes 491528 | tf_op jit(solution)/shard_map/ppermute | solution.py:286
  8.9 0.7 %collective-permute-start.1 = (bf16[128,512]{1,0:T(8,128)(2,1)S(1)}, bf16[128,512]{1,0:T(8,128)(2,1)S(1)}, u32[]{:S(2)}, u32[]{:S(2)}) collective-permute-start(bf16[128,512]{1,0:T(8,128)(2,1)S(1)} %get-tuple-element.22), channel_id=1, source_target_pairs={{1,2},{3,4},{5,6},{7,8},{9,10},{11,12},{13,14},{2,1},{4,3},{6,5},{... | collective-permute-start | bytes 393224 | tf_op jit(solution)/shard_map/ppermute | solution.py:287
  9.6 1.1 %waiting.1 = (f32[512,512]{1,0:T(8,128)S(1)}, bf16[512,512]{1,0:T(8,128)(2,1)S(1)}, f32[1,512]{1,0:T(1,128)S(1)}, f32[1,512]{1,0:T(1,128)S(1)}) custom-call(bf16[512,256]{1,0:T(8,128)(2,1)S(1)} %get-tuple-element.19.adjacency.refs_0_, bf16[256,512]{1,0:T(8,128)(2,1)S(1)} %get-tuple-element.20.state.refs_1_, f32[1,512]{1,0:T(1,128)} %bitcast.3, ...), custom_call_target="tpu_custom_call" | custom-call | flops 1500000000 | bytes 1048576 | tf_op jit(solution)/shard_map/waiting/pallas_call | solution.py:290
  10.7 0.0 collective-permute-done.2.near.refs_4_
  10.7 0.6 %beside.1.near_blocks.refs_7_ = bf16[256,512]{1,0:T(8,128)(2,1)S(1)} custom-call(bf16[128,1152]{1,0:T(8,128)(2,1)S(1)} %collective-permute-done.2.near.refs_4_, f32[512,512]{1,0:T(8,128)S(1)} %get-tuple-element.25.aggregate.refs_10_, bf16[256,512]{1,0:T(8,128)(2,1)S(1)} %get-tuple-element.20.state.refs_1_, ...), custom_call_target="tpu_custom_call" | custom-call | tf_op jit(solution)/shard_map/beside/pallas_call | solution.py:309
  11.3 0.4 %collective-permute-done.3.refs_5_ = bf16[264,512]{1,0:T(8,128)(2,1)S(1)} collective-permute-done((bf16[264,512]{1,0:T(8,128)(2,1)S(1)}, bf16[264,512]{1,0:T(8,128)(2,1)S(1)}, u32[]{:S(2)}, u32[]{:S(2)}) %collective-permute-start.3) | collective-permute-done | bytes 270368 | tf_op jit(solution)/shard_map/ppermute | solution.py:285
  11.7 0.0 collective-permute-start.4
  11.7 0.5 %collective-permute-done.far.refs_2_ = bf16[128,640]{1,0:T(8,128)(2,1)S(1)} collective-permute-done((bf16[128,640]{1,0:T(8,128)(2,1)S(1)}, bf16[128,640]{1,0:T(8,128)(2,1)S(1)}, u32[]{:S(2)}, u32[]{:S(2)}) %collective-permute-start) | collective-permute-done | bytes 163872 | tf_op jit(solution)/shard_map/ppermute | solution.py:286
  12.2 0.8 %apart.1 = (bf16[128,512]{1,0:T(8,128)(2,1)S(1)}, f32[256,512]{1,0:T(8,128)S(1)}) custom-call(bf16[128,640]{1,0:T(8,128)(2,1)S(1)} %collective-permute-done.far.refs_2_, bf16[128,1152]{1,0:T(8,128)(2,1)S(1)} %collective-permute-done.2.near.refs_4_, bf16[256,512]{1,0:T(8,128)(2,1)S(1)} %beside.1.near_blocks.refs_7_, ...), custom_call_target="tpu_custom_call" | custom-call | flops 4000000000 | bytes 1048576 | tf_op jit(solution)/shard_map/apart/pallas_call | solution.py:321
  12.9 0.0 collective-permute-done.1.refs_3_
  13.0 0.3 %collective-permute-done.4.refs_6_ = bf16[264,512]{1,0:T(8,128)(2,1)S(1)} collective-permute-done((bf16[264,512]{1,0:T(8,128)(2,1)S(1)}, bf16[264,512]{1,0:T(8,128)(2,1)S(1)}, u32[]{:S(2)}, u32[]{:S(2)}) %collective-permute-start.4) | collective-permute-done | bytes 270368 | tf_op jit(solution)/shard_map/ppermute | solution.py:319
  13.3 1.5 %layers.1 = f32[1,256]{1,0:T(1,128)} custom-call(bf16[512,256]{1,0:T(8,128)(2,1)S(1)} %get-tuple-element.19.adjacency.refs_0_, bf16[256,512]{1,0:T(8,128)(2,1)S(1)} %get-tuple-element.20.state.refs_1_, bf16[128,640]{1,0:T(8,128)(2,1)S(1)} %collective-permute-done.far.refs_2_, bf16[128,512]{1,0:T(8,128)(2,1)S(1)} %collective-permute-done.1.refs_3_, ...), custom_call_target="tpu_custom_call" | custom-call | tf_op jit(solution)/shard_map/layers/pallas_call | solution.py:335
Async XLA Ops:
  1.5 9.1 %collective-permute-start.2 = (bf16[128,1152]{1,0:T(8,128)(2,1)S(1)}, bf16[128,1152]{1,0:T(8,128)(2,1)S(1)}, u32[]{:S(2)}, u32[]{:S(2)}) collective-permute-start(bf16[128,1152]{1,0:T(8,128)(2,1)S(1)} %get-tuple-element.23), channel_id=1, source_target_pairs={{0,1},{1,0},{2,3},{3,2},{4,5},{5,4},{6,7},{7,6},{8,9},{9,8},{10,11... | collective-permute-start | bytes 884744 | tf_op jit(solution)/shard_map/ppermute | solution.py:288
  2.0 9.7 %collective-permute-start.3 = (bf16[264,512]{1,0:T(8,128)(2,1)S(1)}, bf16[264,512]{1,0:T(8,128)(2,1)S(1)}, u32[]{:S(2)}, u32[]{:S(2)}) collective-permute-start(bf16[264,512]{1,0:T(8,128)(2,1)S(1)} %get-tuple-element.24), channel_id=1, source_target_pairs={{0,16},{16,0},{1,17},{17,1},{2,18},{18,2},{3,19},{19,3},{4,20},{20... | collective-permute-start | bytes 811016 | tf_op jit(solution)/shard_map/ppermute | solution.py:285
  4.6 7.5 %collective-permute-start = (bf16[128,640]{1,0:T(8,128)(2,1)S(1)}, bf16[128,640]{1,0:T(8,128)(2,1)S(1)}, u32[]{:S(2)}, u32[]{:S(2)}) collective-permute-start(bf16[128,640]{1,0:T(8,128)(2,1)S(1)} %get-tuple-element.21), channel_id=1, source_target_pairs={{1,2},{3,4},{5,6},{7,8},{9,10},{11,12},{13,14},{15,0},{2,1},{4,3},... | collective-permute-start | bytes 491528 | tf_op jit(solution)/shard_map/ppermute | solution.py:286
  8.9 4.1 %collective-permute-start.1 = (bf16[128,512]{1,0:T(8,128)(2,1)S(1)}, bf16[128,512]{1,0:T(8,128)(2,1)S(1)}, u32[]{:S(2)}, u32[]{:S(2)}) collective-permute-start(bf16[128,512]{1,0:T(8,128)(2,1)S(1)} %get-tuple-element.22), channel_id=1, source_target_pairs={{1,2},{3,4},{5,6},{7,8},{9,10},{11,12},{13,14},{2,1},{4,3},{6,5},{... | collective-permute-start | bytes 393224 | tf_op jit(solution)/shard_map/ppermute | solution.py:287
  11.7 1.5 %collective-permute-start.4 = (bf16[264,512]{1,0:T(8,128)(2,1)S(1)}, bf16[264,512]{1,0:T(8,128)(2,1)S(1)}, u32[]{:S(2)}, u32[]{:S(2)}) collective-permute-start(bf16[264,512]{1,0:T(8,128)(2,1)S(1)} %collective-permute-done.3.refs_5_), channel_id=1, source_target_pairs={{0,1},{1,0},{2,3},{3,2},{4,5},{5,4},{6,7},{7,6},{8,9},{9,8},{10,11... | collective-permute-start | bytes 811016 | tf_op jit(solution)/shard_map/ppermute | solution.py:319
where the time goes:
time: 14.9 us; the launch traced here: 14.8 us
  starting transfers between devices  8.04 us (54%)
  Pallas kernels  5.55 us (37%)
  waiting for transfers between devices  1.14 us (8%)
    ppermute x1, starting transfers between devices, paired(): far = lax.ppermute(far, 'shard', apart)  4.27 us
    ppermute x1, starting transfers between devices, paired(): crossed = lax.ppermute(crossing, 'section', across)  2.63 us
    pallas_call x1, Pallas kernels, paired(): pl.pallas_call(second_kernel, out_shape=jax.ShapeDtypeStruct((1, rows), F...  1.52 us
    pallas_call x1, Pallas kernels, paired(): pl.pallas_call(first_kernel, out_shape=(jax.ShapeDtypeStruct((size, width...  1.51 us
    pallas_call x1, Pallas kernels, paired(): pl.pallas_call(waiting_kernel, out_shape=(jax.ShapeDtypeStruct((rows + 2...  1.09 us
    pallas_call x1, Pallas kernels, paired(): pl.pallas_call(far_kernel, out_shape=(jax.ShapeDtypeStruct((rows - size,...  0.78 us
    ppermute x1, starting transfers between devices, paired(): lax.ppermute(far_sum, 'shard', [pair for pair in apart if abs(pair[0] - p...  0.66 us
    pallas_call x1, Pallas kernels, paired(): pl.pallas_call(near_kernel, out_shape=jax.ShapeDtypeStruct((2 * size, wid...  0.65 us
  transfers between devices with their start and end apart: 5, of which 3 were waited for; matrix products, arithmetic and copies ran while one was open for 0% of the time, Pallas kernels for 17%

commit v1 on v0

--- a/solution.py
+++ b/solution.py
@@ -43,7 +43,7 @@
 
 def first_kernel(
     tile_rows, tile_cols, tile_live, labels, label_table, tiles, features, gains, weights,
-    far, far_sum, near, crossing, state_out, adjacency_out,
+    far, far_sum, near, near_sum, crossing, state_out, adjacency_out,
     rows_buf, cols_buf, live_buf, labels_buf, classes_buf, tiles_buf, features_buf, gains_buf, table_buf, sums, sems,
 ):
     section = lax.axis_index("section")
@@ -106,9 +106,9 @@
     state = (features_buf[...].astype(F32) + embedded).astype(BF16)
     state_out[...] = state
     partial = dot(adjacency[size : size + rows], state).astype(BF16)
-    near[:, pl.ds(0, width)] = partial[:size]
-    near[:, pl.ds(width, width)] = state[:size]
-    near[:, pl.ds(2 * width, size)] = adjacency[:size, :size]
+    near_sum[...] = partial[:size]
+    near[:, pl.ds(0, width)] = state[:size]
+    near[:, pl.ds(width, size)] = adjacency[:size, :size]
     far_sum[...] = partial[rows - size :]
     far[:, pl.ds(0, width)] = state[rows - size :]
     far[:, pl.ds(width, size)] = adjacency[rows + size :, rows - size :]
@@ -135,12 +135,12 @@
     copies[1].wait()
 
 
-def near_kernel(near, aggregate, state, weight, half_gain, near_blocks):
+def near_kernel(near, near_sum, aggregate, state, weight, half_gain, near_blocks):
     size, width = near.shape[0], aggregate.shape[1]
-    near_state = near[:, pl.ds(width, width)]
+    near_state = near[:, pl.ds(0, width)]
     first, second = pl.ds(0, size), pl.ds(size, size)
-    near_blocks[first, :] = (aggregate[first, :] + near[:, pl.ds(0, width)].astype(F32)).astype(BF16)
-    near_blocks[second, :] = (aggregate[second, :] + dot(near[:, pl.ds(2 * width, size)], near_state)).astype(BF16)
+    near_blocks[first, :] = (aggregate[first, :] + near_sum[...].astype(F32)).astype(BF16)
+    near_blocks[second, :] = (aggregate[second, :] + dot(near[:, pl.ds(width, size)], near_state)).astype(BF16)
 
     @pl.when(lax.axis_index("section") == 0)
     def _():
@@ -167,7 +167,7 @@
         states[pl.ds(0, size), :] = near_blocks[pl.ds(size, size), :]
         states[pl.ds(size, rows - size), :] = far_blocks[...]
         inner[...] = dot(adjacency[pl.ds(size, rows), :], states[...])
-        inner[pl.ds(0, size), :] += dot(near[:, pl.ds(2 * width, size)], near_blocks[pl.ds(0, size), :])
+        inner[pl.ds(0, size), :] += dot(near[:, pl.ds(width, size)], near_blocks[pl.ds(0, size), :])
 
 
 def second_kernel(*refs):
@@ -213,7 +213,7 @@
             source = near_blocks[pl.ds(size, size), :] if start == 0 else far_blocks[pl.ds(start - size, size), :]
             next_states[pl.ds(size + start, size), :] = layer(source, weight[...], gain, state[span, :])
         next_states[pl.ds(0, size), :] = layer(
-            near_blocks[pl.ds(0, size), :], weight[...], gain, near[:, pl.ds(width, width)]
+            near_blocks[pl.ds(0, size), :], weight[...], gain, near[:, pl.ds(0, width)]
         )
     next_states[last, :] = layer(halo, weight[...], gain, far[:, pl.ds(0, width)])
 
@@ -225,7 +225,7 @@
         start = block * size
         summed = inner[start : start + size]
         if block == 0 and not own_first:
-            summed = summed + dot(near[:, pl.ds(2 * width, size)], next_states[pl.ds(0, size), :])
+            summed = summed + dot(near[:, pl.ds(width, size)], next_states[pl.ds(0, size), :])
         if block == rows // size - 1:
             summed = summed + dot(far_tile, next_states[last, :])
         before = next_states[pl.ds(size + start, size), :]
@@ -244,23 +244,23 @@
     depth = weights.shape[1]
     kept = depth // 2
     classes = label_table.shape[0]
-    message = jax.ShapeDtypeStruct((size, 2 * width + size), BF16)
     vmem = pl.BlockSpec(memory_space=pltpu.VMEM)
     hbm = pl.BlockSpec(memory_space=pltpu.HBM)
     table_rows = -(-3 * classes // PAD) * PAD
 
-    far, far_sum, near, crossing, state, adjacency = pl.pallas_call(
+    far, far_sum, near, near_sum, crossing, state, adjacency = pl.pallas_call(
         first_kernel,
         out_shape=(
             jax.ShapeDtypeStruct((size, width + size), BF16),
             jax.ShapeDtypeStruct((size, width), BF16),
-            message,
+            jax.ShapeDtypeStruct((size, width + size), BF16),
+            jax.ShapeDtypeStruct((size, width), BF16),
             jax.ShapeDtypeStruct((kept + EXTRA, width), BF16),
             jax.ShapeDtypeStruct((rows, width), BF16),
             jax.ShapeDtypeStruct((rows + 2 * size, rows), BF16),
         ),
         in_specs=[hbm] * 9,
-        out_specs=(vmem,) * 6,
+        out_specs=(vmem,) * 7,
         scratch_shapes=[
             pltpu.SMEM((groups, slots), jnp.int32),
             pltpu.SMEM((groups, slots), jnp.int32),
@@ -286,6 +286,7 @@
     far = lax.ppermute(far, "shard", apart)
     far_sum = lax.ppermute(far_sum, "shard", [pair for pair in apart if abs(pair[0] - pair[1]) == 1])
     near = lax.ppermute(near, "shard", beside)
+    near_sum = lax.ppermute(near_sum, "shard", beside)
 
     aggregate, own_weight, half_gain, head_row = pl.pallas_call(
         waiting_kernel,
@@ -309,13 +310,13 @@
     near_blocks = pl.pallas_call(
         near_kernel,
         out_shape=jax.ShapeDtypeStruct((2 * size, width), BF16),
-        in_specs=[vmem] * 5,
+        in_specs=[vmem] * 6,
         out_specs=vmem,
         compiler_params=pltpu.CompilerParams(vmem_limit_bytes=16 * 2**20),
         name="beside",
-    )(near, aggregate, state, own_weight, half_gain)
-
-    crossed, near_blocks = lax.optimization_barrier((crossed, near_blocks))
+    )(near, near_sum, aggregate, state, own_weight, half_gain)
+
+    crossed, aggregate = lax.optimization_barrier((crossed, aggregate))
     relayed = lax.ppermute(crossed, "shard", beside)
 
     far_blocks, inner = pl.pallas_call(

time: 14.9 us -> 15.2 us (1.020)
  starting transfers between devices: 8.04 us -> 8.74 us
  waiting for transfers between devices: 1.14 us -> 0.72 us
    ppermute x1, starting transfers between devices: 0.48 us -> 0.01 us  [paired(): near = lax.ppermute(near, 'shard', beside)]
    ppermute x1, waiting for transfers between devices: 0.45 us -> 0.02 us  [paired(): far = lax.ppermute(far, 'shard', apart)]
    ppermute x1, starting transfers between devices: 2.63 us -> 3.03 us  [paired(): crossed = lax.ppermute(crossing, 'section', across)]
    ppermute x1, waiting for transfers between devices: 0.38 us -> 0.01 us  [paired(): crossed = lax.ppermute(crossing, 'section', across)]
    ppermute x1, starting transfers between devices: 4.27 us -> 4.64 us  [paired(): far = lax.ppermute(far, 'shard', apart)]
    ppermute x1, starting transfers between devices: 0.01 us -> 0.34 us  [paired(): relayed = lax.ppermute(crossed, 'shard', beside)]
    ppermute x0 -> x1, waiting for transfers between devices: none -> 0.24 us  [paired(): near_sum = lax.ppermute(near_sum, 'shard', beside)]
    ppermute x1, waiting for transfers between devices: 0.3 us -> 0.46 us  [paired(): relayed = lax.ppermute(crossed, 'shard', beside)]
  transfers between devices with their start and end apart: 5 -> 6, of which waited for: 3 -> 2; matrix products, arithmetic and copies ran while one was open for 0% -> 0% of each run, Pallas kernels for 17% -> 17%
where the time goes in v1:
time: 15.2 us; the launch traced here: 15.1 us
  starting transfers between devices  8.74 us (58%)
  Pallas kernels  5.52 us (36%)
  waiting for transfers between devices  0.72 us (5%)
    ppermute x1, starting transfers between devices, paired(): far = lax.ppermute(far, 'shard', apart)  4.64 us
    ppermute x1, starting transfers between devices, paired(): crossed = lax.ppermute(crossing, 'section', across)  3.03 us
    pallas_call x1, Pallas kernels, paired(): pl.pallas_call(second_kernel, out_shape=jax.ShapeDtypeStruct((1, rows), F...  1.53 us
    pallas_call x1, Pallas kernels, paired(): pl.pallas_call(first_kernel, out_shape=(jax.ShapeDtypeStruct((size, width...  1.48 us
    pallas_call x1, Pallas kernels, paired(): pl.pallas_call(waiting_kernel, out_shape=(jax.ShapeDtypeStruct((rows + 2...  1.09 us
    pallas_call x1, Pallas kernels, paired(): pl.pallas_call(far_kernel, out_shape=(jax.ShapeDtypeStruct((rows - size,...  0.78 us
    ppermute x1, starting transfers between devices, paired(): lax.ppermute(far_sum, 'shard', [pair for pair in apart if abs(pair[0] - p...  0.66 us
    pallas_call x1, Pallas kernels, paired(): pl.pallas_call(near_kernel, out_shape=jax.ShapeDtypeStruct((2 * size, wid...  0.64 us
  transfers between devices with their start and end apart: 6, of which 2 were waited for; matrix products, arithmetic and copies ran while one was open for 0% of the time, Pallas kernels for 17%

profile of v1, /device:TPU:0, one launch (start us, length us, event | category | flops | bytes accessed | tf_op | source)
XLA Modules:
  0.0 15.1 jit_solution(16027331024396364383)
XLA Ops:
  0.0 1.5 %messages.1 = (bf16[128,640]{1,0:T(8,128)(2,1)S(1)}, bf16[128,512]{1,0:T(8,128)(2,1)S(1)}, bf16[128,640]{1,0:T(8,128)(2,1)S(1)}, bf16[128,512]{1,0:T(8,128)(2,1)...) custom-call(s32[2,6]{1,0:T(2,128)} %tile_rows.1, ...), custom_call_target="tpu_custom_call" | custom-call | tf_op jit(solution)/shard_map/messages/pallas_call | solution.py:251
  1.5 3.0 %collective-permute-start.3 = (bf16[264,512]{1,0:T(8,128)(2,1)S(1)}, bf16[264,512]{1,0:T(8,128)(2,1)S(1)}, u32[]{:S(2)}, u32[]{:S(2)}) collective-permute-start(bf16[264,512]{1,0:T(8,128)(2,1)S(1)} %get-tuple-element.25), channel_id=1, source_target_pairs={{0,16},{16,0},{1,17},{17,1},{2,18},{18,2},{3,19},{19,3},{4,20},{20... | collective-permute-start | bytes 811016 | tf_op jit(solution)/shard_map/ppermute | solution.py:285
  4.5 0.0 collective-permute-start.2
  4.5 4.6 %collective-permute-start = (bf16[128,640]{1,0:T(8,128)(2,1)S(1)}, bf16[128,640]{1,0:T(8,128)(2,1)S(1)}, u32[]{:S(2)}, u32[]{:S(2)}) collective-permute-start(bf16[128,640]{1,0:T(8,128)(2,1)S(1)} %get-tuple-element.22), channel_id=1, source_target_pairs={{1,2},{3,4},{5,6},{7,8},{9,10},{11,12},{13,14},{15,0},{2,1},{4,3},... | collective-permute-start | bytes 491528 | tf_op jit(solution)/shard_map/ppermute | solution.py:286
  9.2 0.7 %collective-permute-start.1 = (bf16[128,512]{1,0:T(8,128)(2,1)S(1)}, bf16[128,512]{1,0:T(8,128)(2,1)S(1)}, u32[]{:S(2)}, u32[]{:S(2)}) collective-permute-start(bf16[128,512]{1,0:T(8,128)(2,1)S(1)} %get-tuple-element.23), channel_id=1, source_target_pairs={{1,2},{3,4},{5,6},{7,8},{9,10},{11,12},{13,14},{2,1},{4,3},{6,5},{... | collective-permute-start | bytes 393224 | tf_op jit(solution)/shard_map/ppermute | solution.py:287
  9.8 0.1 collective-permute-start.5
  9.9 1.1 %waiting.1 = (f32[512,512]{1,0:T(8,128)S(1)}, bf16[512,512]{1,0:T(8,128)(2,1)S(1)}, f32[1,512]{1,0:T(1,128)S(1)}, f32[1,512]{1,0:T(1,128)S(1)}) custom-call(bf16[512,256]{1,0:T(8,128)(2,1)S(1)} %get-tuple-element.20.adjacency.refs_0_, bf16[256,512]{1,0:T(8,128)(2,1)S(1)} %get-tuple-element.21.state.refs_1_, f32[1,512]{1,0:T(1,128)} %bitcast.3, ...), custom_call_target="tpu_custom_call" | custom-call | flops 1500000000 | bytes 1048576 | tf_op jit(solution)/shard_map/waiting/pallas_call | solution.py:291
  11.0 0.2 %collective-permute-done.5.near_sum = bf16[128,512]{1,0:T(8,128)(2,1)S(1)} collective-permute-done((bf16[128,512]{1,0:T(8,128)(2,1)S(1)}, bf16[128,512]{1,0:T(8,128)(2,1)S(1)}, u32[]{:S(2)}, u32[]{:S(2)}) %collective-permute-start.5) | collective-permute-done | bytes 131104 | tf_op jit(solution)/shard_map/ppermute | solution.py:289
  11.2 0.0 collective-permute-done.2.near.refs_4_
  11.2 0.6 %beside.1.near_blocks.refs_7_ = bf16[256,512]{1,0:T(8,128)(2,1)S(1)} custom-call(bf16[128,640]{1,0:T(8,128)(2,1)S(1)} %collective-permute-done.2.near.refs_4_, bf16[128,512]{1,0:T(8,128)(2,1)S(1)} %collective-permute-done.5.near_sum, f32[512,512]{1,0:T(8,128)S(1)} %get-tuple-element.31.aggregate.refs_10_, ...), custom_call_target="tpu_custom_call" | custom-call | tf_op jit(solution)/shard_map/beside/pallas_call | solution.py:310
  11.9 0.0 collective-permute-done.3.refs_5_
  11.9 0.3 %collective-permute-start.4 = (bf16[264,512]{1,0:T(8,128)(2,1)S(1)}, bf16[264,512]{1,0:T(8,128)(2,1)S(1)}, u32[]{:S(2)}, u32[]{:S(2)}) collective-permute-start(bf16[264,512]{1,0:T(8,128)(2,1)S(1)} %collective-permute-done.3.refs_5_), channel_id=1, source_target_pairs={{0,1},{1,0},{2,3},{3,2},{4,5},{5,4},{6,7},{7,6},{8,9},{9,8},{10,11... | collective-permute-start | bytes 811016 | tf_op jit(solution)/shard_map/ppermute | solution.py:320
  12.2 0.0 collective-permute-done.far.refs_2_
  12.3 0.8 %apart.1 = (bf16[128,512]{1,0:T(8,128)(2,1)S(1)}, f32[256,512]{1,0:T(8,128)S(1)}) custom-call(bf16[128,640]{1,0:T(8,128)(2,1)S(1)} %collective-permute-done.far.refs_2_, bf16[128,640]{1,0:T(8,128)(2,1)S(1)} %collective-permute-done.2.near.refs_4_, bf16[256,512]{1,0:T(8,128)(2,1)S(1)} %beside.1.near_blocks.refs_7_, ...), custom_call_target="tpu_custom_call" | custom-call | flops 4000000000 | bytes 1048576 | tf_op jit(solution)/shard_map/apart/pallas_call | solution.py:322
  13.1 0.0 collective-permute-done.1.refs_3_
  13.1 0.5 %collective-permute-done.4.refs_6_ = bf16[264,512]{1,0:T(8,128)(2,1)S(1)} collective-permute-done((bf16[264,512]{1,0:T(8,128)(2,1)S(1)}, bf16[264,512]{1,0:T(8,128)(2,1)S(1)}, u32[]{:S(2)}, u32[]{:S(2)}) %collective-permute-start.4) | collective-permute-done | bytes 270368 | tf_op jit(solution)/shard_map/ppermute | solution.py:320
  13.5 1.5 %layers.1 = f32[1,256]{1,0:T(1,128)} custom-call(bf16[512,256]{1,0:T(8,128)(2,1)S(1)} %get-tuple-element.20.adjacency.refs_0_, bf16[256,512]{1,0:T(8,128)(2,1)S(1)} %get-tuple-element.21.state.refs_1_, bf16[128,640]{1,0:T(8,128)(2,1)S(1)} %collective-permute-done.far.refs_2_, bf16[128,512]{1,0:T(8,128)(2,1)S(1)} %collective-permute-done.1.refs_3_, ...), custom_call_target="tpu_custom_call" | custom-call | tf_op jit(solution)/shard_map/layers/pallas_call | solution.py:336
Async XLA Ops:
  1.5 10.4 %collective-permute-start.3 = (bf16[264,512]{1,0:T(8,128)(2,1)S(1)}, bf16[264,512]{1,0:T(8,128)(2,1)S(1)}, u32[]{:S(2)}, u32[]{:S(2)}) collective-permute-start(bf16[264,512]{1,0:T(8,128)(2,1)S(1)} %get-tuple-element.25), channel_id=1, source_target_pairs={{0,16},{16,0},{1,17},{17,1},{2,18},{18,2},{3,19},{19,3},{4,20},{20... | collective-permute-start | bytes 811016 | tf_op jit(solution)/shard_map/ppermute | solution.py:285
  4.5 6.7 %collective-permute-start.2 = (bf16[128,640]{1,0:T(8,128)(2,1)S(1)}, bf16[128,640]{1,0:T(8,128)(2,1)S(1)}, u32[]{:S(2)}, u32[]{:S(2)}) collective-permute-start(bf16[128,640]{1,0:T(8,128)(2,1)S(1)} %get-tuple-element.24), channel_id=1, source_target_pairs={{0,1},{1,0},{2,3},{3,2},{4,5},{5,4},{6,7},{7,6},{8,9},{9,8},{10,11... | collective-permute-start | bytes 491528 | tf_op jit(solution)/shard_map/ppermute | solution.py:288
  4.5 7.7 %collective-permute-start = (bf16[128,640]{1,0:T(8,128)(2,1)S(1)}, bf16[128,640]{1,0:T(8,128)(2,1)S(1)}, u32[]{:S(2)}, u32[]{:S(2)}) collective-permute-start(bf16[128,640]{1,0:T(8,128)(2,1)S(1)} %get-tuple-element.22), channel_id=1, source_target_pairs={{1,2},{3,4},{5,6},{7,8},{9,10},{11,12},{13,14},{15,0},{2,1},{4,3},... | collective-permute-start | bytes 491528 | tf_op jit(solution)/shard_map/ppermute | solution.py:286
  9.2 3.9 %collective-permute-start.1 = (bf16[128,512]{1,0:T(8,128)(2,1)S(1)}, bf16[128,512]{1,0:T(8,128)(2,1)S(1)}, u32[]{:S(2)}, u32[]{:S(2)}) collective-permute-start(bf16[128,512]{1,0:T(8,128)(2,1)S(1)} %get-tuple-element.23), channel_id=1, source_target_pairs={{1,2},{3,4},{5,6},{7,8},{9,10},{11,12},{13,14},{2,1},{4,3},{6,5},{... | collective-permute-start | bytes 393224 | tf_op jit(solution)/shard_map/ppermute | solution.py:287
  9.8 1.4 %collective-permute-start.5 = (bf16[128,512]{1,0:T(8,128)(2,1)S(1)}, bf16[128,512]{1,0:T(8,128)(2,1)S(1)}, u32[]{:S(2)}, u32[]{:S(2)}) collective-permute-start(bf16[128,512]{1,0:T(8,128)(2,1)S(1)} %get-tuple-element.28), channel_id=1, source_target_pairs={{0,1},{1,0},{2,3},{3,2},{4,5},{5,4},{6,7},{7,6},{8,9},{9,8},{10,11... | collective-permute-start | bytes 393224 | tf_op jit(solution)/shard_map/ppermute | solution.py:289
  11.9 1.6 %collective-permute-start.4 = (bf16[264,512]{1,0:T(8,128)(2,1)S(1)}, bf16[264,512]{1,0:T(8,128)(2,1)S(1)}, u32[]{:S(2)}, u32[]{:S(2)}) collective-permute-start(bf16[264,512]{1,0:T(8,128)(2,1)S(1)} %collective-permute-done.3.refs_5_), channel_id=1, source_target_pairs={{0,1},{1,0},{2,3},{3,2},{4,5},{5,4},{6,7},{7,6},{8,9},{9,8},{10,11... | collective-permute-start | bytes 811016 | tf_op jit(solution)/shard_map/ppermute | solution.py:320
